TPU v7x, 1024 devices: a whole 8x8x8 slice. The times are simulated.
1024 devices in a mesh: ep: 64 (over z, y), tp: 16 (over x, core).
Axes of the slice: x: 8, y: 8, z: 8, core: 2. Of those that a mesh axis runs over, the one named last changes fastest.
Arguments:
- tokens: bfloat16 [2048, 3200], P('ep', 'tp'), may hold values from -6 to 6
- grad_out: bfloat16 [2048, 3200], P('ep', 'tp'), may hold values from -6 to 6
- route_weight: float32 [2048], P('ep'), may hold values from 0.1 to 1
- routes: int32 [2048, 1], P('ep'), may hold values from 0 to 15, as said below
- gate_weight: bfloat16 [64, 2288, 3200], P('ep', 'tp'), may hold values from -0.109375 to 0.109375
- up_weight: bfloat16 [64, 2288, 3200], P('ep', 'tp'), may hold values from -0.109375 to 0.109375
- down_weight: bfloat16 [64, 2288, 3200], P('ep', 'tp'), may hold values from -0.0625 to 0.0625
Outputs:
- grad_in: bfloat16 [2048, 3200], P('ep', 'tp')
Inputs may be any that keep to these rules, and one draw needn't show every extreme that they name: `routes`: each token names one expert. In every device's block of 32 tokens (aligned blocks along the token dimension) no expert is named more than 4 times, and one expert, the same for all blocks, is named exactly 4 times in every block.
All inputs are finite; a program needn't handle non-finite values.
Results may differ from a plain program's by a relative error of at most 0.0049.
Values may be sent and summed in bfloat16 or wider, within the bound.
A program may use at most 32 MiB of HBM per device.

v0:
```python
import jax
import jax.numpy as jnp
from jax import lax
from jax.sharding import PartitionSpec as P

GROUP = 4


def per_device(tokens, grad_out, route_weight, routes, gate_weight, up_weight, down_weight):
    ep_size = lax.axis_size("ep")
    experts = ep_size // GROUP
    tok_rows = tokens.shape[0]
    capacity = GROUP * (min(2 * tok_rows * GROUP // ep_size, 3 * tok_rows // 4) // GROUP)
    w_gate = gate_weight[0]
    w_up = up_weight[0]
    w_down = down_weight[0]
    expert_of = routes[:, 0]
    onehot = (expert_of[:, None] == jnp.arange(experts, dtype=jnp.int32)[None, :]).astype(jnp.int32)
    rank_inside = jnp.sum(jnp.cumsum(onehot, axis=0) * onehot, axis=1) - 1
    slot_ids = expert_of * capacity + rank_inside
    placement = (
        slot_ids[None, :] == jnp.arange(experts * capacity, dtype=jnp.int32)[:, None]
    ).astype(jnp.bfloat16)
    paired = jnp.stack([tokens, grad_out])
    feat_width = paired.shape[2]
    packed = jnp.einsum(
        "st,ktw->ksw", placement, paired, preferred_element_type=jnp.float32
    ).astype(jnp.bfloat16)
    packed = packed.reshape(2, experts, capacity, feat_width)
    outgoing = jnp.broadcast_to(
        packed[:, :, None], (2, experts, GROUP, capacity, feat_width)
    ).reshape(2, ep_size, capacity, feat_width)
    arrived = lax.all_to_all(outgoing, "ep", split_axis=1, concat_axis=1, tiled=True)
    slot_rows = arrived.reshape(2, ep_size * capacity, feat_width)
    contract = (((1,), (1,)), ((), ()))
    piece_pair = lax.all_gather(slot_rows, "tp", axis=2, tiled=True)
    cols_gate = w_gate
    cols_up = w_up
    gate_sum = lax.dot_general(
        piece_pair[0], cols_gate, contract, preferred_element_type=jnp.float32
    )
    up_sum = lax.dot_general(piece_pair[0], cols_up, contract, preferred_element_type=jnp.float32)
    down_sum = lax.dot_general(piece_pair[1], w_down, contract, preferred_element_type=jnp.float32)
    sigmoid_gate = jax.nn.sigmoid(gate_sum)
    up_grad = (down_sum * gate_sum * sigmoid_gate).astype(jnp.bfloat16)
    gate_grad = (down_sum * up_sum * sigmoid_gate * (1.0 + gate_sum * (1.0 - sigmoid_gate))).astype(
        jnp.bfloat16
    )
    out_width = tokens.shape[1]
    flip_dims = (((0,), (1,)), ((), ()))
    cols_gate = w_gate
    cols_up = w_up
    summed = lax.psum_scatter(
        lax.dot_general(cols_gate, gate_grad, flip_dims, preferred_element_type=jnp.float32)
        + lax.dot_general(cols_up, up_grad, flip_dims, preferred_element_type=jnp.float32),
        "tp",
        scatter_dimension=0,
        tiled=True,
    )
    partial_value = summed.T
    returned = lax.all_to_all(
        partial_value.reshape(ep_size, capacity, out_width),
        "ep",
        split_axis=0,
        concat_axis=0,
        tiled=True,
    )
    merged = jnp.sum(returned.reshape(experts, GROUP, capacity, out_width), axis=1).reshape(
        experts * capacity, out_width
    )
    total_grad = jnp.take(merged, slot_ids, axis=0)
    return (route_weight[:, None] * total_grad).astype(jnp.bfloat16)


def solution(mesh):
    return jax.shard_map(
        per_device,
        mesh=mesh,
        in_specs=(
            P("ep", "tp"),
            P("ep", "tp"),
            P("ep"),
            P("ep", None),
            P("ep", "tp", None),
            P("ep", "tp", None),
            P("ep", "tp", None),
        ),
        out_specs=P("ep", "tp"),
        check_vma=False,
    )
```

profile of v0, /device:TPU:14, one launch (start us, length us, event | category | flops | bytes accessed | tf_op | source)
XLA Modules:
  0.0 231.3 jit_solution(13543185932451747652)
XLA Ops:
  6.5 0.8 fusion.37
  7.4 0.8 select_reduce_fusion
  8.2 0.7 multiply_add_fusion
  8.9 1.0 fusion.22
  9.9 0.1 copy.14
  10.0 0.1 broadcast_in_dim.23
  10.1 38.1 %all_to_all.10 = bf16[2,64,4,200]{3,0,2,1:T(2,128)(2,1)S(1)} all-to-all(bf16[2,64,4,200]{3,0,2,1:T(2,128)(2,1)S(1)} %bitcast.58), channel_id=1, replica_groups=mesh['ep'=64,'tp'=16] {'ep'}, dimensions={1} | all-to-all | bytes 409600 | tf_op jit(solution)/shard_map/all_to_all | solution.py:33
  48.3 1.0 copy.11
  49.3 37.8 %all-gather.2.cloned.1.call-done = bf16[2,256,3200]{1,0,2:T(2,128)(2,1)} async-done(((bf16[2,256,200]{1,0,2:T(2,128)(2,1)}), bf16[2,256,3200]{1,0,2:T(2,128)(2,1)}) %all-gather.2.cloned.1.call-update) | async-done | bytes 3276816 | tf_op jit(solution)/shard_map/all_gather | solution.py:36
  87.1 9.8 %fusion.44 = (bf16[1,256,3200]{1,0,2:T(2,128)(2,1)}, bf16[1,256,3200]{1,0,2:T(2,128)(2,1)}) fusion(bf16[2,256,3200]{1,0,2:T(2,128)(2,1)} %all-gather.2.cloned.1.call-done), kind=kLoop, calls=%fused_computation.47 | loop fusion | bytes 6553600 | tf_op jit(solution)/shard_map/slice | solution.py:42
  96.9 6.1 %copy.18 = bf16[1,256,3200]{2,1,0:T(8,128)(2,1)S(1)} copy(bf16[1,256,3200]{1,0,2:T(2,128)(2,1)} %get-tuple-element.7) | data formatting | bytes 3276800
  103.0 7.5 %copy.17 = bf16[1,256,3200]{2,1,0:T(8,128)(2,1)} copy(bf16[1,256,3200]{1,0,2:T(2,128)(2,1)} %get-tuple-element.8) | data formatting | bytes 3276800
  110.5 1.3 fusion.1
  111.8 3.0 %fusion.5 = f32[256,143]{0,1:T(8,128)} fusion(bf16[1,256,3200]{2,1,0:T(8,128)(2,1)} %copy.17, bf16[1,143,3200]{2,1,0:T(8,128)(2,1)} %param.13), kind=kOutput, calls=%fused_computation.7 | convolution fusion | flops 234291200 | bytes 2700032 | tf_op jit(solution)/shard_map/dot_general | solution.py:43
  114.9 4.8 %fusion.20 = f32[256,3200]{1,0:T(8,128)} fusion(f32[256,143]{0,1:T(8,128)} %fusion.5, bf16[1,256,3200]{2,1,0:T(8,128)(2,1)S(1)} %copy.18, bf16[1,143,3200]{2,1,0:T(8,128)(2,1)S(1)} %copy-done.1, bf16[1,143,3200]{2,1,0:T(8,128)(2,1)S(1)} %copy-done, f32[256,143]{0,1:T(8,128)} %fusion.1), kind=kOutput, calls=%fused_computation.14 | convolution fusion | flops 468948480 | bytes 7038464 | tf_op jit(solution)/shard_map/dot_general | solution.py:54
  119.7 4.5 %fusion = f32[3200,256]{0,1:T(8,128)} fusion(f32[256,3200]{1,0:T(8,128)} %fusion.20, bf16[1,143,3200]{2,1,0:T(8,128)(2,1)S(1)} %copy-done, f32[256,143]{0,1:T(8,128)} %fusion.5, f32[256,143]{0,1:T(8,128)} %fusion.1), kind=kOutput, calls=%fused_computation.2 | convolution fusion | flops 235330048 | bytes 7761664 | tf_op jit(solution)/shard_map/dot_general | solution.py:55
  124.1 4.8 %copy.15 = f32[3200,256]{1,0:T(8,128)} copy(f32[3200,256]{0,1:T(8,128)} %fusion) | data formatting | bytes 6553600
  129.0 63.0 %reduce-scatter.4.cloned.1.call-done = f32[200,256]{1,0:T(8,128)} async-done(((f32[3200,256]{1,0:T(8,128)}), f32[200,256]{1,0:T(8,128)}) %reduce-scatter.4.cloned.1.call-update) | async-done | bytes 204816
  192.0 1.1 copy.16
  193.0 0.8 reshape.42
  193.8 14.0 %all-to-all-start.1 = ((f32[64,4,200]{2,1,0:T(4,128)}), f32[64,4,200]{2,1,0:T(4,128)S(1)}, u32[]{:S(2)}, u32[]{:S(2)}) async-start(f32[64,4,200]{2,1,0:T(4,128)} %reshape.42), calls=%async_computation.1 | async-start | bytes 524288 | tf_op jit(solution)/shard_map/all_to_all | solution.py:61
  207.9 15.2 %all-to-all-done.1 = f32[64,4,200]{2,1,0:T(4,128)S(1)} async-done(((f32[64,4,200]{2,1,0:T(4,128)}), f32[64,4,200]{2,1,0:T(4,128)S(1)}, u32[]{:S(2)}, u32[]{:S(2)}) %all-to-all-start.1) | async-done | bytes 204832 | tf_op jit(solution)/shard_map/all_to_all | solution.py:61
  223.2 0.6 gather_fusion
  223.8 0.7 multiply_convert_fusion.2
  (17 shorter events, 0.2 us)
Async XLA Ops:
  6.5 108.3 %copy-start = (bf16[1,143,3200]{2,1,0:T(8,128)(2,1)S(1)}, bf16[1,143,3200]{2,1,0:T(8,128)(2,1)}, u32[]{:S(2)}) copy-start(bf16[1,143,3200]{2,1,0:T(8,128)(2,1)} %param.12) | copy-start | bytes 2745604
  6.5 80.6 %all-gather.2.cloned.1.call-start = ((), (), s32[]{:S(2)}) async-start(), calls=%async_computation.3 | async-start | bytes 3481600 | tf_op jit(solution)/shard_map/all_gather | solution.py:36
  49.2 142.7 %reduce-scatter.4.cloned.1.call-start = ((), (), s32[]{:S(2)}) async-start(), calls=%async_computation.4 | async-start | bytes 3481600
  103.0 7.5 %copy-start.1 = (bf16[1,143,3200]{2,1,0:T(8,128)(2,1)S(1)}, bf16[1,143,3200]{2,1,0:T(8,128)(2,1)}, u32[]{:S(2)}) copy-start(bf16[1,143,3200]{2,1,0:T(8,128)(2,1)} %param.11) | copy-start | bytes 2745604
  128.9 78.9 %copy-start.2 = (s32[32,1]{0,1:T(1,128)S(1)}, s32[32,1]{0,1:T(1,128)}, u32[]{:S(2)}) copy-start(s32[32,1]{0,1:T(1,128)} %param.10) | copy-start | bytes 388
  129.0 94.8 %copy-start.3 = (f32[32]{0:T(128)S(1)}, f32[32]{0:T(128)}, u32[]{:S(2)}) copy-start(f32[32]{0:T(128)} %param.9) | copy-start | bytes 388
  193.8 29.3 %all-to-all-start.1 = ((f32[64,4,200]{2,1,0:T(4,128)}), f32[64,4,200]{2,1,0:T(4,128)S(1)}, u32[]{:S(2)}, u32[]{:S(2)}) async-start(f32[64,4,200]{2,1,0:T(4,128)} %reshape.42), calls=%async_computation.1 | async-start | bytes 524288 | tf_op jit(solution)/shard_map/all_to_all | solution.py:61
Sparse Core Ops, SparseCore 0:
  49.4 37.7 all-gather.1
  129.1 62.8 reduce-scatter.3
where the time goes:
time: 233 us; the launch traced here: 231 us
  waiting for transfers between devices  116 us (50%)
  blocking collectives  38.1 us (16%)
  local copies, waits for them, and re-layouts  31.8 us (14%)
  matrix products  14.6 us (6%)
  starting transfers between devices  14.1 us (6%)
  between operations  13.5 us (6%)
  other arithmetic  3.11 us (1%)
    unnamed x3, waiting for transfers between devices  63 us
    all_to_all x1, blocking collectives, per_device(): lax.all_to_all(outgoing, 'ep', split_axis=1, concat_axis=1, tiled=True)  38.1 us
    all_gather x1, waiting for transfers between devices, per_device(): piece_pair = lax.all_gather(slot_rows, 'tp', axis=2, tiled=True)  37.8 us
    unnamed x12, local copies, waits for them, and re-layouts  19.5 us
    all_to_all x1, waiting for transfers between devices, per_device(): lax.all_to_all(partial_value.reshape(ep_size, capacity, out_width), 'ep',...  15.2 us
    all_to_all x1, starting transfers between devices, per_device(): lax.all_to_all(partial_value.reshape(ep_size, capacity, out_width), 'ep',...  14 us
    slice x1, local copies, waits for them, and re-layouts, per_device(): piece_pair[0]  9.79 us
    dot_general x1, matrix products, per_device(): lax.dot_general(cols_gate, gate_grad, flip_dims, preferred_element_type=j...  4.81 us
  transfers between devices with their start and end apart: 3, of which 3 were waited for; matrix products, arithmetic and copies ran while one was open for 0% of the time, Pallas kernels for 0%

commit v1 on v0

v1 whole, which is shorter than its diff:
```python
import functools

import jax
import jax.numpy as jnp
from jax import lax
from jax.experimental import pallas as pl
from jax.experimental.pallas import tpu as pltpu
from jax.sharding import PartitionSpec as P

NZ = 8
NY = 8
NX = 8
HALF = 4
CAP = 4
LANES = 128
WIDE = 256
BF = jnp.bfloat16
F32 = jnp.float32
NN = (((1,), (0,)), ((), ()))
TN = (((0,), (0,)), ((), ()))


def iota(shape, dim):
    return lax.broadcasted_iota(jnp.int32, shape, dim)


def hops(half, way):
    return 4 if half == way else 3


def kernel(
    tok, grd, weight, routes, gate_hbm, up_hbm, down_hbm, out,
    w_gate, w_up, w_down, w_sem,
    z_out, z_in, y_out, y_in, acts, part, twin, chain_out, chain_in,
    back_out, back_in, last_out, last_in,
    zs, zr, ys, yr, gs, gr, bs, br, ps, pr, cs, cr, us, ur, vs, vr,
):
    ep = lax.axis_index("ep")
    tp = lax.axis_index("tp")
    z, y = ep // NY, ep % NY
    x, c = tp // 2, tp % 2
    h, yy = y // HALF, y % HALF
    feat = tok.shape[1]
    hid = w_gate.shape[1]
    rows = part.shape[3]
    chip = 2 * feat

    def at(zz, yv, xx, cc):
        return {"ep": zz * NY + yv, "tp": xx * 2 + cc}

    def remote(src, dst, send, recv, where):
        return pltpu.make_async_remote_copy(
            src_ref=src, dst_ref=dst, send_sem=send, recv_sem=recv,
            device_id=where, device_id_type=pl.DeviceIdType.MESH,
        )

    def y_of(i):
        hh = h if i < HALF else 1 - h
        return hh, (yy + i) % HALF

    loads = []
    for n, (src, dst) in enumerate(((gate_hbm, w_gate), (up_hbm, w_up), (down_hbm, w_down))):
        load = pltpu.make_async_copy(src, dst, w_sem.at[n])
        load.start()
        loads.append(load)

    barrier = pltpu.get_barrier_semaphore()
    greeted = [at((z + k) % NZ, y, x, c) for k in range(1, NZ)]
    for i in range(NY):
        hh, yv = y_of(i)
        if i > 0:
            greeted.append(at(z, hh * HALF + yv, x, c))
        greeted.append(at(z, hh * HALF + yv, x, 1 - c))
    greeted.append(at(z, y, (x + 1) % NX, c))
    greeted.append(at(z, y, (x + NX - 1) % NX, c))
    for where in greeted:
        pl.semaphore_signal(barrier, inc=1, device_id=where, device_id_type=pl.DeviceIdType.MESH)

    n_tok = tok.shape[0]
    n_slot = NZ * 2 * CAP
    row_i, col_i = iota((n_tok, n_tok), 0), iota((n_tok, n_tok), 1)
    diag = row_i == col_i

    def column(v):
        return jnp.sum(jnp.where(diag, v, 0.0), axis=1, keepdims=True)

    r_row = routes[...].astype(F32)
    r_col = column(jnp.broadcast_to(r_row, (n_tok, n_tok)))
    same = jnp.where((r_col == r_row) & (row_i < col_i), 1.0, 0.0)
    slot_row = r_row * CAP + jnp.sum(same, axis=0, keepdims=True)
    slot_col = column(jnp.broadcast_to(slot_row, (n_tok, n_tok)))
    w_col = column(jnp.broadcast_to(weight[...], (n_tok, n_tok)))
    p_row = iota((2 * n_slot, n_tok), 0)
    p_slot = ((p_row // (2 * CAP)) * CAP + p_row % CAP).astype(F32)
    p_arr = (p_row // CAP) % 2
    hit = p_slot == slot_row
    put_x = jnp.where(hit & (p_arr == 0), 1.0, 0.0).astype(BF)
    put_g = jnp.where(hit & (p_arr == 1), 1.0, 0.0).astype(BF)
    packed = lax.dot_general(put_x, tok[...], NN, preferred_element_type=F32)
    packed += lax.dot_general(put_g, grd[...], NN, preferred_element_type=F32)
    packed = jnp.concatenate([packed, jnp.zeros((2 * n_slot, WIDE - feat), F32)], axis=1)
    z_out[...] = packed.astype(BF).reshape(z_out.shape)

    pl.semaphore_wait(barrier, len(greeted))

    z_copies = []
    for k in range(1, NZ):
        zd = (z + k) % NZ
        copy = remote(z_out.at[zd], z_in.at[z], zs.at[k - 1], zr.at[k - 1], at(zd, y, x, c))
        copy.start()
        z_copies.append(copy)
    z_in[z] = z_out[z]
    for load in loads:
        load.wait()
    for copy in z_copies:
        copy.wait_recv()

    n_in = 2 * n_slot
    q_out, q_in = iota((n_in, n_in), 0), iota((n_in, n_in), 1)
    per = NZ * CAP
    want = ((q_out % per) // CAP) * (4 * CAP) + (q_out // per) * CAP + q_out % CAP
    perm = jnp.where(q_in == want, 1.0, 0.0).astype(BF)
    moved = lax.dot_general(perm, z_in[...].reshape(n_in, WIDE), NN, preferred_element_type=F32)
    y_out[...] = moved.astype(BF).reshape(y_out.shape)

    y_copies = {}
    for i in range(NY):
        hh, yv = y_of(i)
        for o in range(2):
            if i == 0 and o == 0:
                continue
            cc = (c + o) % 2
            copy = remote(
                y_out.at[hh, cc], y_in.at[c, (i // HALF) * HALF + yy],
                ys.at[i, o], yr.at[i, o], at(z, hh * HALF + yv, x, cc),
            )
            copy.start()
            y_copies[i, o] = copy
    y_in[c, yy] = y_out[h, c]

    right, left = (x + 1) % NX, (x + NX - 1) % NX
    g_copies, b_copies = {}, {}

    def piece(j, way, s):
        return (x + NX - s) % NX if way == 0 else (x + s) % NX

    def hand_over(j, n, p):
        copy = remote(
            acts.at[c, j, p], acts.at[c, j, p], bs.at[j, n], br.at[j, n], at(z, y, x, 1 - c)
        )
        copy.start()
        b_copies[j, n] = copy

    def forward(j, way, s):
        p = piece(j, way, s)
        copy = remote(
            acts.at[c, j, p], acts.at[c, j, p], gs.at[j, way, s], gr.at[j, way, s],
            at(z, y, right if way == 0 else left, c),
        )
        copy.start()
        g_copies[j, way, s] = copy

    def begin(j):
        for i in range(j * HALF, j * HALF + HALF):
            for o in range(2):
                if (i, o) in y_copies:
                    y_copies[i, o].wait_recv()
        halves = []
        for core in range(2):
            block = y_in[core, j * HALF:(j + 1) * HALF].reshape(LANES, WIDE)
            halves.append(block.astype(F32).T[:feat])
        acts[c, j, x] = jnp.concatenate(halves, axis=0).astype(BF)
        forward(j, 0, 0)
        forward(j, 1, 0)
        hand_over(j, 0, x)

    def arrive(j, s):
        for way in range(2):
            if s > hops(j, way):
                continue
            g_copies[j, way, s - 1].wait_recv()
            if s < hops(j, way):
                forward(j, way, s)
            hand_over(j, s if way == 0 else hops(j, 0) + s, piece(j, way, s))

    def compute(j):
        for n in range(NX):
            b_copies[j, n].wait_recv()
        xs = acts[0, j].reshape(NX * chip, LANES)
        dy = acts[1, j].reshape(NX * chip, LANES)
        gate = lax.dot_general(w_gate[0], xs, NN, preferred_element_type=F32)
        up = lax.dot_general(w_up[0], xs, NN, preferred_element_type=F32)
        down = lax.dot_general(w_down[0], dy, NN, preferred_element_type=F32)
        sig = 1.0 / (1.0 + jnp.exp(-gate))
        up_grad = (down * gate * sig).astype(BF)
        gate_grad = (down * up * sig * (1.0 + gate * (1.0 - sig))).astype(BF)
        res = lax.dot_general(w_gate[0], gate_grad, TN, preferred_element_type=F32)
        res += lax.dot_general(w_up[0], up_grad, TN, preferred_element_type=F32)
        fill = jnp.zeros((rows - feat, LANES), F32)
        for px in range(NX):
            for pc in range(2):
                lo = px * chip + pc * feat
                part[j, pc, px] = jnp.concatenate([res[lo:lo + feat], fill], axis=0).astype(BF)
        copy = remote(part.at[j, 1 - c], twin.at[j], ps.at[j], pr.at[j], at(z, y, x, 1 - c))
        copy.start()
        return copy

    def own(j, d):
        return part[j, c, d].astype(F32) + twin[j, d].astype(F32)

    c_copies = {}

    def link(j, way, t):
        n = hops(j, way)
        d = (x + n - t) % NX if way == 0 else (x + NX - n + t) % NX
        val = own(j, d)
        if t > 0:
            c_copies[j, way, t - 1].wait_recv()
            val += chain_in[j, way, t - 1].astype(F32)
        chain_out[j, way, t] = val.astype(BF)
        copy = remote(
            chain_out.at[j, way, t], chain_in.at[j, way, t], cs.at[j, way, t], cr.at[j, way, t],
            at(z, y, right if way == 0 else left, c),
        )
        copy.start()
        c_copies[j, way, t] = copy

    u_copies = {}

    def give_back(j):
        val = own(j, x)
        for way in range(2):
            n = hops(j, way)
            c_copies[j, way, n - 1].wait_recv()
            val += chain_in[j, way, n - 1].astype(F32)
        val = jnp.concatenate([val, jnp.zeros((WIDE - rows, LANES), F32)], axis=0)
        back_out[j] = val.T.astype(BF).reshape(back_out.shape[1:])
        for i in range(j * HALF, j * HALF + HALF):
            hh, yv = y_of(i)
            if i == 0:
                continue
            copy = remote(
                back_out.at[j, yv], back_in.at[j * HALF + yy], us.at[i], ur.at[i],
                at(z, hh * HALF + yv, x, c),
            )
            copy.start()
            u_copies[i] = copy
        if j == 0:
            back_in[yy] = back_out[0, yy]

    begin(0)
    begin(1)
    for s in range(1, 4):
        arrive(0, s)
        arrive(1, s)
    arrive(0, 4)
    arrive(1, 4)
    p_copies = [compute(0), compute(1)]
    for j in range(2):
        p_copies[j].wait_recv()
        link(j, 0, 0)
        link(j, 1, 0)
    for t in range(1, 4):
        for j in range(2):
            for way in range(2):
                if t < hops(j, way):
                    link(j, way, t)
    give_back(0)
    give_back(1)

    sums = []
    for j in range(2):
        for i in range(j * HALF, j * HALF + HALF):
            if i > 0:
                u_copies[i].wait_recv()
        total = back_in[j * HALF].astype(F32)
        for n in range(1, HALF):
            total += back_in[j * HALF + n].astype(F32)
        sums.append(total)
    both = jnp.concatenate(sums, axis=0)
    v_out, v_in = iota((n_slot, n_slot), 0), iota((n_slot, n_slot), 1)
    half = (v_out // CAP) % 2
    rel = (half + h) % 2
    src = rel * per + (v_out // (2 * CAP)) * CAP + v_out % CAP
    turn = jnp.where(v_in == src, 1.0, 0.0)
    last_out[...] = lax.dot_general(
        turn, both, NN, precision=lax.Precision.HIGHEST, preferred_element_type=F32
    ).reshape(last_out.shape)
    v_copies = []
    for k in range(1, NZ):
        zd = (z + k) % NZ
        copy = remote(last_out.at[zd], last_in.at[z], vs.at[k - 1], vr.at[k - 1], at(zd, y, x, c))
        copy.start()
        v_copies.append(copy)
    last_in[z] = last_out[z]
    pick = jnp.where(slot_col == iota((n_tok, n_slot), 1).astype(F32), 1.0, 0.0)
    for copy in v_copies:
        copy.wait_recv()
    got = lax.dot_general(
        pick, last_in[...].reshape(n_slot, WIDE), NN,
        precision=lax.Precision.HIGHEST, preferred_element_type=F32,
    )
    out[...] = (w_col * got[:, :feat]).astype(BF)

    for group in (z_copies, y_copies.values(), g_copies.values(), b_copies.values(), p_copies,
                  c_copies.values(), u_copies.values(), v_copies):
        for copy in group:
            copy.wait_send()


def per_device(tokens, grad_out, route_weight, routes, gate_weight, up_weight, down_weight):
    n_tok, feat = tokens.shape
    _, hid, width = gate_weight.shape
    rows = -(-feat // 16) * 16
    vmem = pl.BlockSpec(memory_space=pltpu.VMEM)
    hbm = pl.BlockSpec(memory_space=pl.ANY)
    dma = pltpu.SemaphoreType.DMA
    n_slot = NZ * 2 * CAP
    return pl.pallas_call(
        kernel,
        out_shape=jax.ShapeDtypeStruct((n_tok, feat), BF),
        in_specs=[vmem, vmem, vmem, vmem, hbm, hbm, hbm],
        out_specs=vmem,
        scratch_shapes=[
            pltpu.VMEM((1, hid, width), BF),
            pltpu.VMEM((1, hid, width), BF),
            pltpu.VMEM((1, hid, width), BF),
            dma((3,)),
            pltpu.VMEM((NZ, 4 * CAP, WIDE), BF),
            pltpu.VMEM((NZ, 4 * CAP, WIDE), BF),
            pltpu.VMEM((2, 2, NZ * CAP, WIDE), BF),
            pltpu.VMEM((2, NY, NZ * CAP, WIDE), BF),
            pltpu.VMEM((2, 2, NX, 2 * feat, LANES), BF),
            pltpu.VMEM((2, 2, NX, rows, LANES), BF),
            pltpu.VMEM((2, NX, rows, LANES), BF),
            pltpu.VMEM((2, 2, 4, rows, LANES), BF),
            pltpu.VMEM((2, 2, 4, rows, LANES), BF),
            pltpu.VMEM((2, HALF, NZ * CAP, WIDE), BF),
            pltpu.VMEM((NY, NZ * CAP, WIDE), BF),
            pltpu.VMEM((NZ, 2 * CAP, WIDE), F32),
            pltpu.VMEM((NZ, 2 * CAP, WIDE), F32),
            dma((NZ - 1,)), dma((NZ - 1,)),
            dma((NY, 2)), dma((NY, 2)),
            dma((2, 2, 4)), dma((2, 2, 4)),
            dma((2, NX)), dma((2, NX)),
            dma((2,)), dma((2,)),
            dma((2, 2, 4)), dma((2, 2, 4)),
            dma((NY,)), dma((NY,)),
            dma((NZ - 1,)), dma((NZ - 1,)),
        ],
        compiler_params=pltpu.CompilerParams(
            collective_id=0, has_side_effects=True, vmem_limit_bytes=40 * 1024 * 1024
        ),
    )(
        tokens, grad_out, route_weight.reshape(1, n_tok), routes.reshape(1, n_tok),
        gate_weight, up_weight, down_weight,
    )


def solution(mesh):
    return jax.shard_map(
        per_device,
        mesh=mesh,
        in_specs=(
            P("ep", "tp"),
            P("ep", "tp"),
            P("ep"),
            P("ep", None),
            P("ep", "tp", None),
            P("ep", "tp", None),
            P("ep", "tp", None),
        ),
        out_specs=P("ep", "tp"),
        check_vma=False,
    )
```

time: 233 us -> 92.8 us (0.40)
  waiting for transfers between devices: 116 us -> 0 us
  Pallas kernels: 0 us -> 86.2 us
  blocking collectives: 38.1 us -> 0 us
  local copies, waits for them, and re-layouts: 31.8 us -> 6.25 us
  matrix products: 14.6 us -> 0 us
  starting transfers between devices: 14.1 us -> 0 us
  between operations: 13.5 us -> 0.02 us
  other arithmetic: 3.11 us -> 0 us
    pallas_call x0 -> x1, Pallas kernels: none -> 86.2 us  [per_device(): pl.pallas_call(kernel, out_shape=jax.ShapeDtypeStruct((n_tok, feat), BF),...]
    unnamed x3 -> x0, waiting for transfers between devices: 63 us -> none
    all_to_all x1 -> x0, blocking collectives: 38.1 us -> none  [per_device(): lax.all_to_all(outgoing, 'ep', split_axis=1, concat_axis=1, tiled=True)]
    all_gather x1 -> x0, waiting for transfers between devices: 37.8 us -> none  [per_device(): piece_pair = lax.all_gather(slot_rows, 'tp', axis=2, tiled=True)]
    all_to_all x1 -> x0, waiting for transfers between devices: 15.2 us -> none  [per_device(): lax.all_to_all(partial_value.reshape(ep_size, capacity, out_width), 'ep',...]
    dot_general x5 -> x0, matrix products: 14.6 us -> none  [the longest x1 4.81 us: per_device(): lax.dot_general(cols_gate, gate_grad, flip_dims, preferred_element_type=j...]
    all_to_all x1 -> x0, starting transfers between devices: 14 us -> none  [per_device(): lax.all_to_all(partial_value.reshape(ep_size, capacity, out_width), 'ep',...]
    unnamed x12 -> x15, local copies, waits for them, and re-layouts: 19.5 us -> 6.25 us
  transfers between devices with their start and end apart: 3 -> 0, of which waited for: 3 -> 0; matrix products, arithmetic and copies ran while one was open for 0% -> 0% of each run, Pallas kernels for 0% -> 0%
where the time goes in v1:
time: 92.8 us; the launch traced here: 92.5 us
  Pallas kernels  86.2 us (93%)
  local copies, waits for them, and re-layouts  6.25 us (7%)
    pallas_call x1, Pallas kernels, per_device(): pl.pallas_call(kernel, out_shape=jax.ShapeDtypeStruct((n_tok, feat), BF),...  86.2 us
    unnamed x15, local copies, waits for them, and re-layouts  6.25 us

profile of v1, /device:TPU:14, one launch (start us, length us, event | category | flops | bytes accessed | tf_op | source)
XLA Modules:
  0.0 92.5 jit_solution(14529423330277337844)
XLA Ops:
  0.0 0.0 copy-start.5
  0.0 0.0 copy-start.6
  0.0 0.7 copy-done.5
  0.7 0.0 copy-done.6
  0.7 0.0 copy-start
  0.7 1.2 %copy-done = bf16[1,143,3200]{2,1,0:T(8,128)(2,1)S(1)} copy-done((bf16[1,143,3200]{2,1,0:T(8,128)(2,1)S(1)}, bf16[1,143,3200]{2,1,0:T(8,128)(2,1)}, u32[]{:S(2)}) %copy-start) | copy-done | bytes 915224
  1.9 0.0 copy-start.1
  1.9 1.2 %copy-done.1 = bf16[1,143,3200]{2,1,0:T(8,128)(2,1)S(1)} copy-done((bf16[1,143,3200]{2,1,0:T(8,128)(2,1)S(1)}, bf16[1,143,3200]{2,1,0:T(8,128)(2,1)}, u32[]{:S(2)}) %copy-start.1) | copy-done | bytes 915224
  3.0 0.0 copy-start.2
  3.0 1.2 %copy-done.2 = bf16[1,143,3200]{2,1,0:T(8,128)(2,1)S(1)} copy-done((bf16[1,143,3200]{2,1,0:T(8,128)(2,1)S(1)}, bf16[1,143,3200]{2,1,0:T(8,128)(2,1)}, u32[]{:S(2)}) %copy-start.2) | copy-done | bytes 915224
  4.2 0.0 copy-start.3
  4.2 0.7 copy-done.3
  4.9 0.0 copy-start.4
  4.9 0.7 copy-done.4
  5.7 86.2 %shard_map.73 = bf16[32,200]{1,0:T(8,128)(2,1)S(1)} custom-call(bf16[32,200]{1,0:T(8,128)(2,1)S(1)} %copy-done.3, bf16[32,200]{1,0:T(8,128)(2,1)S(1)} %copy-done.4, f32[1,32]{1,0:T(1,128)S(1)} %bitcast.2, s32[1,32]{1,0:T(1,128)S(1)} %bitcast.3, bf16[1,143,3200]{2,1,0:T(8,128)(2,1)S(1)} %copy-done, bf16[1,143,3200]{2,1,0:T(8,128)(2,1)S(1)} %copy-done.1, ...), custom_call_target="tpu_custom_call" | custom-call | tf_op jit(solution)/shard_map/pallas_call | solution.py:319
  91.9 0.6 copy.9
Async XLA Ops:
  0.0 0.7 copy-start.5
  0.0 0.7 copy-start.6
  0.7 1.2 %copy-start = (bf16[1,143,3200]{2,1,0:T(8,128)(2,1)S(1)}, bf16[1,143,3200]{2,1,0:T(8,128)(2,1)}, u32[]{:S(2)}) copy-start(bf16[1,143,3200]{2,1,0:T(8,128)(2,1)} %gate_hbm.1) | copy-start | bytes 2745604
  1.9 1.2 %copy-start.1 = (bf16[1,143,3200]{2,1,0:T(8,128)(2,1)S(1)}, bf16[1,143,3200]{2,1,0:T(8,128)(2,1)}, u32[]{:S(2)}) copy-start(bf16[1,143,3200]{2,1,0:T(8,128)(2,1)} %up_hbm.1) | copy-start | bytes 2745604
  3.0 1.2 %copy-start.2 = (bf16[1,143,3200]{2,1,0:T(8,128)(2,1)S(1)}, bf16[1,143,3200]{2,1,0:T(8,128)(2,1)}, u32[]{:S(2)}) copy-start(bf16[1,143,3200]{2,1,0:T(8,128)(2,1)} %down_hbm.1) | copy-start | bytes 2745604
  4.2 0.7 copy-start.3
  4.9 0.7 copy-start.4

commit v2 on v1

v2 whole, which is shorter than its diff:
```python
import functools

import jax
import jax.numpy as jnp
from jax import lax
from jax.experimental import pallas as pl
from jax.experimental.pallas import tpu as pltpu
from jax.sharding import PartitionSpec as P

NZ = 8
NY = 8
NX = 8
HALF = 4
CAP = 4
LANES = 128
WIDE = 256
BF = jnp.bfloat16
F32 = jnp.float32
NN = (((1,), (0,)), ((), ()))
TN = (((0,), (0,)), ((), ()))


G_CUT = (208, 192)
C_CUT = (112, 96)
FAR = NX // 2
STEPS = 3
ORDER = ((0, FAR), (0, 3), (1, 3), (0, 2), (1, 2), (0, 1), (1, 1), (0, 0))


def iota(shape, dim):
    return lax.broadcasted_iota(jnp.int32, shape, dim)


def kernel(
    tok_hbm, grd_hbm, weight_hbm, routes_hbm, gate_hbm, up_hbm, down_hbm, out,
    tok, grd, weight, routes, w_gate, w_up, w_down, w_sem,
    t_gate, t_up, z_out, z_in, y_out, y_in, f_out, f_in, acts, keep, part, twin, chain_out, chain_in,
    back_out, back_in, far_out, far_in, sum_out, sum_in, last_out, last_in,
    zs, zr, ys, yr, fs, fr, ws, wr, gs, gr, bs, br, ps, pr, cs, cr, us, ur, ks, kr, es, er, vs, vr,
):
    ep = lax.axis_index("ep")
    tp = lax.axis_index("tp")
    z, y = ep // NY, ep % NY
    x, c = tp // 2, tp % 2
    h, yy = y // HALF, y % HALF
    feat = tok.shape[1]
    rows = part.shape[2]
    chip = 2 * feat

    def at(zz, yv, xx, cc):
        return {"ep": zz * NY + yv, "tp": xx * 2 + cc}

    started = []

    def remote(src, dst, send, recv, where):
        copy = pltpu.make_async_remote_copy(
            src_ref=src, dst_ref=dst, send_sem=send, recv_sem=recv,
            device_id=where, device_id_type=pl.DeviceIdType.MESH,
        )
        copy.start()
        started.append(copy)
        return copy

    def y_of(i):
        hh = h if i < HALF else 1 - h
        return hh, (yy + i) % HALF

    loads = []
    for n, (src, dst) in enumerate((
        (routes_hbm, routes), (tok_hbm, tok), (grd_hbm, grd), (weight_hbm, weight),
        (gate_hbm, w_gate), (up_hbm, w_up), (down_hbm, w_down),
    )):
        load = pltpu.make_async_copy(src, dst, w_sem.at[n])
        load.start()
        loads.append(load)

    barrier = pltpu.get_barrier_semaphore()
    greeted = [at((z + k) % NZ, y, x, c) for k in range(1, NZ)]
    for i in range(NY):
        hh, yv = y_of(i)
        if i > 0:
            greeted.append(at(z, hh * HALF + yv, x, c))
        greeted.append(at(z, hh * HALF + yv, x, 1 - c))
    greeted.append(at(z, y, (x + FAR) % NX, c))
    greeted.append(at(z, y, (x + 1) % NX, c))
    greeted.append(at(z, y, (x + NX - 1) % NX, c))
    for where in greeted:
        pl.semaphore_signal(barrier, inc=1, device_id=where, device_id_type=pl.DeviceIdType.MESH)

    for load in loads[:4]:
        load.wait()
    n_tok = tok.shape[0]
    n_slot = NZ * 2 * CAP
    row_i, col_i = iota((n_tok, n_tok), 0), iota((n_tok, n_tok), 1)
    diag = row_i == col_i

    def column(v):
        return jnp.sum(jnp.where(diag, v, 0.0), axis=1, keepdims=True)

    r_row = routes[...].astype(F32)
    r_col = column(jnp.broadcast_to(r_row, (n_tok, n_tok)))
    same = jnp.where((r_col == r_row) & (row_i < col_i), 1.0, 0.0)
    slot_row = r_row * CAP + jnp.sum(same, axis=0, keepdims=True)
    slot_col = column(jnp.broadcast_to(slot_row, (n_tok, n_tok)))
    w_col = column(jnp.broadcast_to(weight[...], (n_tok, n_tok)))
    p_row = iota((2 * n_slot, n_tok), 0)
    p_slot = ((p_row // (2 * CAP)) * CAP + p_row % CAP).astype(F32)
    p_arr = (p_row // CAP) % 2
    hit = p_slot == slot_row
    put_x = jnp.where(hit & (p_arr == 0), 1.0, 0.0).astype(BF)
    put_g = jnp.where(hit & (p_arr == 1), 1.0, 0.0).astype(BF)
    packed = lax.dot_general(put_x, tok[...], NN, preferred_element_type=F32)
    packed += lax.dot_general(put_g, grd[...], NN, preferred_element_type=F32)
    packed = jnp.concatenate([packed, jnp.zeros((2 * n_slot, WIDE - feat), F32)], axis=1)
    z_out[...] = packed.astype(BF).reshape(z_out.shape)

    pl.semaphore_wait(barrier, len(greeted))

    z_copies = []
    for k in range(1, NZ):
        zd = (z + k) % NZ
        copy = remote(z_out.at[zd], z_in.at[z], zs.at[k - 1], zr.at[k - 1], at(zd, y, x, c))
        z_copies.append(copy)
    z_in[z] = z_out[z]
    for load in loads[4:]:
        load.wait()
    hid = w_gate.shape[1]
    unit = jnp.where(iota((hid, hid), 0) == iota((hid, hid), 1), 1.0, 0.0).astype(BF)

    def transpose(src, dst):
        res = lax.dot_general(src[0], unit, TN, preferred_element_type=F32)
        dst[...] = res.astype(BF).reshape(dst.shape)

    transpose(w_gate, t_gate)
    for copy in z_copies:
        copy.wait_recv()

    n_in = 2 * n_slot
    q_out, q_in = iota((n_in, n_in), 0), iota((n_in, n_in), 1)
    per = NZ * CAP
    want = ((q_out % per) // CAP) * (4 * CAP) + (q_out // per) * CAP + q_out % CAP
    perm = jnp.where(q_in == want, 1.0, 0.0).astype(BF)
    moved = lax.dot_general(perm, z_in[...].reshape(n_in, WIDE), NN, preferred_element_type=F32)
    y_out[...] = moved.astype(BF).reshape(y_out.shape)

    def spread(src, dst, send, recv):
        copies = {}
        for i in range(NY):
            hh, yv = y_of(i)
            for o in range(2):
                if i == 0 and o == 0:
                    continue
                cc = (c + o) % 2
                copies[i, o] = remote(
                    src.at[hh, cc], dst.at[c, (i // HALF) * HALF + yy],
                    send.at[i, o], recv.at[i, o], at(z, hh * HALF + yv, x, cc),
                )
        dst[c, yy] = src[h, c]
        return copies

    opposite = (x + FAR) % NX
    f_copy = remote(y_out, f_out, fs.at[0], fr.at[0], at(z, y, opposite, c))
    y_copies = spread(y_out, y_in, ys, yr)
    transpose(w_up, t_up)

    right, left = (x + 1) % NX, (x + NX - 1) % NX
    g_copies, b_copies = {}, {}

    def target(way, dist):
        return (x + dist) % NX if way == 0 else (x + NX - dist) % NX

    def cut(parts, n):
        lo = sum(parts[:n])
        return pl.ds(lo, parts[n])

    def hand_over(j, n, p, m):
        rest = acts.at[c, j, p, cut(G_CUT, m)]
        b_copies[j, n, m] = remote(rest, rest, bs.at[j, n, m], br.at[j, n, m], at(z, y, x, 1 - c))

    def forward(j, way, s, m):
        piece = acts.at[c, j, target(1 - way, s), cut(G_CUT, m)]
        g_copies[j, way, s, m] = remote(
            piece, piece, gs.at[j, way, s, m], gr.at[j, way, s, m],
            at(z, y, right if way == 0 else left, c),
        )

    def prepare(j, copies, src, p):
        for i in range(j * HALF, j * HALF + HALF):
            for o in range(2):
                if (i, o) in copies:
                    copies[i, o].wait_recv()
        halves = []
        for core in range(2):
            block = src[core, j * HALF:(j + 1) * HALF].reshape(LANES, WIDE)
            halves.append(block.astype(F32).T[:feat])
        acts[c, j, p] = jnp.concatenate(halves, axis=0).astype(BF)

    def begin(j):
        for m in range(len(G_CUT)):
            forward(j, 0, 0, m)
            forward(j, 1, 0, m)
        for m in range(len(G_CUT)):
            hand_over(j, 0, x, m)

    def arrive(j, s):
        for m in range(len(G_CUT)):
            for way in range(2):
                g_copies[j, way, s - 1, m].wait_recv()
                if s < STEPS:
                    forward(j, way, s, m)
                hand_over(j, s if way == 0 else STEPS + s, target(1 - way, s), m)

    def multiply():
        for copy in b_copies.values():
            copy.wait_recv()

        def both(a):
            return jnp.concatenate([acts[a, j].reshape(NX * chip, LANES) for j in range(2)], axis=1)

        xs, dy = both(0), both(1)
        gate = lax.dot_general(w_gate[0], xs, NN, preferred_element_type=F32)
        up = lax.dot_general(w_up[0], xs, NN, preferred_element_type=F32)
        down = lax.dot_general(w_down[0], dy, NN, preferred_element_type=F32)
        sig = 1.0 / (1.0 + jnp.exp(-gate))
        up_grad = (down * gate * sig).astype(BF)
        gate_grad = (down * up * sig * (1.0 + gate * (1.0 - sig))).astype(BF)
        return gate_grad, up_grad

    p_copies = {}

    def partials(gate_grad, up_grad):
        fill = jnp.zeros((rows - feat, LANES), F32)
        for n, (way, dist) in enumerate(ORDER):
            d = target(way, dist)
            res = lax.dot_general(t_gate[d], gate_grad, NN, preferred_element_type=F32)
            res += lax.dot_general(t_up[d], up_grad, NN, preferred_element_type=F32)
            for j in range(2):
                here = res[:, j * LANES:(j + 1) * LANES]
                low = jnp.concatenate([here[:feat], fill], axis=0)
                high = jnp.concatenate([here[feat:], fill], axis=0)
                keep[d, j] = jnp.where(c == 0, low, high)
                part[d, j] = jnp.where(c == 0, high, low).astype(BF)
            p_copies[way, dist] = remote(
                part.at[d], twin.at[d], ps.at[n], pr.at[n], at(z, y, x, 1 - c)
            )

    met = set()

    def own(j, way, dist):
        key = (0, 0) if dist == 0 else (way, dist)
        if key not in met:
            met.add(key)
            p_copies[key].wait_recv()
        d = target(way, dist)
        return keep[d, j] + twin[d, j].astype(F32)

    c_copies = {}

    def link(j, way, t):
        val = own(j, way, STEPS - t)
        for m in range(len(C_CUT)):
            here = cut(C_CUT, m)
            lo, hi = sum(C_CUT[:m]), sum(C_CUT[:m + 1])
            send = val[lo:hi]
            if t > 0:
                c_copies[j, way, t - 1, m].wait_recv()
                send += chain_in[j, way, t - 1, lo:hi].astype(F32)
            chain_out[j, way, t, lo:hi] = send.astype(BF)
            c_copies[j, way, t, m] = remote(
                chain_out.at[j, way, t, here], chain_in.at[j, way, t, here],
                cs.at[j, way, t, m], cr.at[j, way, t, m],
                at(z, y, right if way == 0 else left, c),
            )

    def give_back(j, val, src, dst, send, recv, copies):
        val = jnp.concatenate([val, jnp.zeros((WIDE - rows, LANES), F32)], axis=0)
        src[j] = val.T.astype(BF).reshape(src.shape[1:])
        for i in range(j * HALF, j * HALF + HALF):
            hh, yv = y_of(i)
            if i == 0:
                continue
            copies[i] = remote(
                src.at[j, yv], dst.at[j * HALF + yy], send.at[i], recv.at[i],
                at(z, hh * HALF + yv, x, c),
            )
        if j == 0:
            dst[yy] = src[0, yy]

    def collect(src, copies):
        sums = []
        for j in range(2):
            for i in range(j * HALF, j * HALF + HALF):
                if i > 0:
                    copies[i].wait_recv()
            total = src[j * HALF].astype(F32)
            for n in range(1, HALF):
                total += src[j * HALF + n].astype(F32)
            sums.append(total)
        return jnp.concatenate(sums, axis=0)

    prepare(0, y_copies, y_in, x)
    begin(0)
    f_copy.wait_recv()
    f_copies = spread(f_out, f_in, ws, wr)
    prepare(1, y_copies, y_in, x)
    begin(1)
    for s in range(1, STEPS + 1):
        for j in range(2):
            arrive(j, s)
        if s == 2:
            for j in range(2):
                prepare(j, f_copies, f_in, opposite)
                for m in range(len(G_CUT)):
                    hand_over(j, NX - 1, opposite, m)
    partials(*multiply())
    k_copies = {}
    for j in range(2):
        give_back(j, own(j, 0, FAR), far_out, far_in, ks, kr, k_copies)
    for t in range(STEPS):
        for j in range(2):
            link(j, j, t)
            link(j, 1 - j, t)
    sum_out[...] = collect(far_in, k_copies).astype(BF)
    e_copy = remote(sum_out, sum_in, es.at[0], er.at[0], at(z, y, opposite, c))
    u_copies = {}
    for j in range(2):
        val = own(j, 0, 0)
        for way in range(2):
            for m in range(len(C_CUT)):
                c_copies[j, way, STEPS - 1, m].wait_recv()
            val += chain_in[j, way, STEPS - 1].astype(F32)
        give_back(j, val, back_out, back_in, us, ur, u_copies)
    both = collect(back_in, u_copies)
    e_copy.wait_recv()
    both += sum_in[...].astype(F32)

    v_out, v_in = iota((n_slot, n_slot), 0), iota((n_slot, n_slot), 1)
    half = (v_out // CAP) % 2
    rel = (half + h) % 2
    src = rel * per + (v_out // (2 * CAP)) * CAP + v_out % CAP
    turn = jnp.where(v_in == src, 1.0, 0.0)
    last_out[...] = lax.dot_general(
        turn, both, NN, precision=lax.Precision.HIGHEST, preferred_element_type=F32
    ).reshape(last_out.shape)
    v_copies = []
    for k in range(1, NZ):
        zd = (z + k) % NZ
        copy = remote(last_out.at[zd], last_in.at[z], vs.at[k - 1], vr.at[k - 1], at(zd, y, x, c))
        v_copies.append(copy)
    last_in[z] = last_out[z]
    pick = jnp.where(slot_col == iota((n_tok, n_slot), 1).astype(F32), 1.0, 0.0)
    for copy in v_copies:
        copy.wait_recv()
    got = lax.dot_general(
        pick, last_in[...].reshape(n_slot, WIDE), NN,
        precision=lax.Precision.HIGHEST, preferred_element_type=F32,
    )
    out[...] = (w_col * got[:, :feat]).astype(BF)

    for copy in started:
        copy.wait_send()


def per_device(tokens, grad_out, route_weight, routes, gate_weight, up_weight, down_weight):
    n_tok, feat = tokens.shape
    _, hid, width = gate_weight.shape
    rows = -(-feat // 16) * 16
    vmem = pl.BlockSpec(memory_space=pltpu.VMEM)
    hbm = pl.BlockSpec(memory_space=pl.ANY)
    dma = pltpu.SemaphoreType.DMA
    n_slot = NZ * 2 * CAP
    return pl.pallas_call(
        kernel,
        out_shape=jax.ShapeDtypeStruct((n_tok, feat), BF),
        in_specs=[hbm] * 7,
        out_specs=vmem,
        scratch_shapes=[
            pltpu.VMEM((n_tok, feat), BF),
            pltpu.VMEM((n_tok, feat), BF),
            pltpu.VMEM((1, n_tok), F32),
            pltpu.VMEM((1, n_tok), jnp.int32),
            pltpu.VMEM((1, hid, width), BF),
            pltpu.VMEM((1, hid, width), BF),
            pltpu.VMEM((1, hid, width), BF),
            dma((7,)),
            pltpu.VMEM((NX, 2 * feat, hid), BF),
            pltpu.VMEM((NX, 2 * feat, hid), BF),
            pltpu.VMEM((NZ, 4 * CAP, WIDE), BF),
            pltpu.VMEM((NZ, 4 * CAP, WIDE), BF),
            pltpu.VMEM((2, 2, NZ * CAP, WIDE), BF),
            pltpu.VMEM((2, NY, NZ * CAP, WIDE), BF),
            pltpu.VMEM((2, 2, NZ * CAP, WIDE), BF),
            pltpu.VMEM((2, NY, NZ * CAP, WIDE), BF),
            pltpu.VMEM((2, 2, NX, 2 * feat, LANES), BF),
            pltpu.VMEM((NX, 2, rows, LANES), F32),
            pltpu.VMEM((NX, 2, rows, LANES), BF),
            pltpu.VMEM((NX, 2, rows, LANES), BF),
            pltpu.VMEM((2, 2, STEPS, rows, LANES), BF),
            pltpu.VMEM((2, 2, STEPS, rows, LANES), BF),
            pltpu.VMEM((2, HALF, NZ * CAP, WIDE), BF),
            pltpu.VMEM((NY, NZ * CAP, WIDE), BF),
            pltpu.VMEM((2, HALF, NZ * CAP, WIDE), BF),
            pltpu.VMEM((NY, NZ * CAP, WIDE), BF),
            pltpu.VMEM((2 * NZ * CAP, WIDE), BF),
            pltpu.VMEM((2 * NZ * CAP, WIDE), BF),
            pltpu.VMEM((NZ, 2 * CAP, WIDE), F32),
            pltpu.VMEM((NZ, 2 * CAP, WIDE), F32),
            dma((NZ - 1,)), dma((NZ - 1,)),
            dma((NY, 2)), dma((NY, 2)),
            dma((1,)), dma((1,)),
            dma((NY, 2)), dma((NY, 2)),
            dma((2, 2, STEPS, 2)), dma((2, 2, STEPS, 2)),
            dma((2, NX, 2)), dma((2, NX, 2)),
            dma((NX,)), dma((NX,)),
            dma((2, 2, STEPS, 2)), dma((2, 2, STEPS, 2)),
            dma((NY,)), dma((NY,)),
            dma((NY,)), dma((NY,)),
            dma((1,)), dma((1,)),
            dma((NZ - 1,)), dma((NZ - 1,)),
        ],
        compiler_params=pltpu.CompilerParams(
            collective_id=0, has_side_effects=True, vmem_limit_bytes=60 * 1024 * 1024
        ),
    )(
        tokens, grad_out, route_weight.reshape(1, n_tok), routes.reshape(1, n_tok),
        gate_weight, up_weight, down_weight,
    )


def solution(mesh):
    return jax.shard_map(
        per_device,
        mesh=mesh,
        in_specs=(
            P("ep", "tp"),
            P("ep", "tp"),
            P("ep"),
            P("ep", None),
            P("ep", "tp", None),
            P("ep", "tp", None),
            P("ep", "tp", None),
        ),
        out_specs=P("ep", "tp"),
        check_vma=False,
    )
```

time: 92.8 us -> 81.9 us (0.88)
  the two profiles are of different devices: /device:TPU:14 before, /device:TPU:16 now
where the time goes in v2:
time: 81.9 us; the launch traced here: 81.7 us
  Pallas kernels  80.4 us (98%)
  local copies, waits for them, and re-layouts  1.32 us (2%)
    pallas_call x1, Pallas kernels, per_device(): pl.pallas_call(kernel, out_shape=jax.ShapeDtypeStruct((n_tok, feat), BF),...  80.4 us

profile of v2, /device:TPU:16, one launch (start us, length us, event | category | flops | bytes accessed | tf_op | source)
XLA Modules:
  0.0 81.7 jit_solution(7918303744839182174)
XLA Ops:
  0.0 80.4 %shard_map.73 = bf16[32,200]{1,0:T(8,128)(2,1)} custom-call(bf16[32,200]{1,0:T(8,128)(2,1)} %tok_hbm.1, bf16[32,200]{1,0:T(8,128)(2,1)} %grd_hbm.1, f32[1,32]{1,0:T(1,128)} %bitcast.2, s32[1,32]{1,0:T(1,128)} %bitcast.3, bf16[1,143,3200]{2,1,0:T(8,128)(2,1)} %gate_hbm.1, bf16[1,143,3200]{2,1,0:T(8,128)(2,1)} %up_hbm.1, bf16[1,143,3200]{2,1,0:T(8,128)(2,1)} %down_hbm.1), custom_call_target="tpu_custom_call" | custom-call | tf_op jit(solution)/shard_map/pallas_call | solution.py:372
  80.4 1.3 %copy.9 = bf16[32,200]{1,0:T(8,128)(2,1)} copy(bf16[32,200]{1,0:T(8,128)(2,1)} %shard_map.73) | data formatting | bytes 25600

commit v3 on v2

--- a/solution.py
+++ b/solution.py
@@ -24,7 +24,7 @@
 C_CUT = (112, 96)
 FAR = NX // 2
 STEPS = 3
-ORDER = ((0, FAR), (0, 3), (1, 3), (0, 2), (1, 2), (0, 1), (1, 1), (0, 0))
+ORDER = ((0, 3), (1, 3), (0, FAR), (0, 2), (1, 2), (0, 1), (1, 1), (0, 0))
 
 
 def iota(shape, dim):
@@ -34,9 +34,9 @@
 def kernel(
     tok_hbm, grd_hbm, weight_hbm, routes_hbm, gate_hbm, up_hbm, down_hbm, out,
     tok, grd, weight, routes, w_gate, w_up, w_down, w_sem,
-    t_gate, t_up, z_out, z_in, y_out, y_in, f_out, f_in, acts, keep, part, twin, chain_out, chain_in,
+    t_gate, t_up, w_cut, pre, z_out, z_in, y_out, y_in, f_out, h_in, h_out, f_in, acts, keep, part, twin, chain_out, chain_in,
     back_out, back_in, far_out, far_in, sum_out, sum_in, last_out, last_in,
-    zs, zr, ys, yr, fs, fr, ws, wr, gs, gr, bs, br, ps, pr, cs, cr, us, ur, ks, kr, es, er, vs, vr,
+    zs, zr, ys, yr, fs, fr, hs, hr, ws, wr, gs, gr, bs, br, ps, pr, cs, cr, us, ur, ks, kr, es, er, vs, vr,
 ):
     ep = lax.axis_index("ep")
     tp = lax.axis_index("tp")
@@ -64,15 +64,6 @@
     def y_of(i):
         hh = h if i < HALF else 1 - h
         return hh, (yy + i) % HALF
-
-    loads = []
-    for n, (src, dst) in enumerate((
-        (routes_hbm, routes), (tok_hbm, tok), (grd_hbm, grd), (weight_hbm, weight),
-        (gate_hbm, w_gate), (up_hbm, w_up), (down_hbm, w_down),
-    )):
-        load = pltpu.make_async_copy(src, dst, w_sem.at[n])
-        load.start()
-        loads.append(load)
 
     barrier = pltpu.get_barrier_semaphore()
     greeted = [at((z + k) % NZ, y, x, c) for k in range(1, NZ)]
@@ -86,6 +77,15 @@
     greeted.append(at(z, y, (x + NX - 1) % NX, c))
     for where in greeted:
         pl.semaphore_signal(barrier, inc=1, device_id=where, device_id_type=pl.DeviceIdType.MESH)
+
+    loads = []
+    for n, (src, dst) in enumerate((
+        (routes_hbm, routes), (tok_hbm, tok), (grd_hbm, grd), (weight_hbm, weight),
+        (gate_hbm, w_gate), (up_hbm, w_up), (down_hbm, w_down),
+    )):
+        load = pltpu.make_async_copy(src, dst, w_sem.at[n])
+        load.start()
+        loads.append(load)
 
     for load in loads[:4]:
         load.wait()
@@ -116,12 +116,19 @@
 
     pl.semaphore_wait(barrier, len(greeted))
 
-    z_copies = []
-    for k in range(1, NZ):
-        zd = (z + k) % NZ
-        copy = remote(z_out.at[zd], z_in.at[z], zs.at[k - 1], zr.at[k - 1], at(zd, y, x, c))
-        z_copies.append(copy)
-    z_in[z] = z_out[z]
+    def to_z(src, dst, send, recv):
+        copies = []
+        for k in range(1, NZ):
+            zd = (z + k) % NZ
+            copies.append(
+                remote(src.at[zd], dst.at[z], send.at[k - 1], recv.at[k - 1], at(zd, y, x, c))
+            )
+        dst[z] = src[z]
+        return copies
+
+    z_copies = to_z(z_out, z_in, zs, zr)
+    opposite = (x + FAR) % NX
+    f_copy = remote(z_out, f_out, fs.at[0], fr.at[0], at(z, y, opposite, c))
     for load in loads[4:]:
         load.wait()
     hid = w_gate.shape[1]
@@ -129,19 +136,31 @@
 
     def transpose(src, dst):
         res = lax.dot_general(src[0], unit, TN, preferred_element_type=F32)
-        dst[...] = res.astype(BF).reshape(dst.shape)
+        for p in range(NX):
+            low = res[p * chip:p * chip + feat]
+            high = res[p * chip + feat:(p + 1) * chip]
+            dst[p, 0] = jnp.where(c == 0, low, high).astype(BF)
+            dst[p, 1] = jnp.where(c == 0, high, low).astype(BF)
+
+    def cut_up(n, src):
+        for p in range(NX):
+            w_cut[n, p] = src[0, :, p * chip:(p + 1) * chip]
 
     transpose(w_gate, t_gate)
-    for copy in z_copies:
-        copy.wait_recv()
-
+    cut_up(0, w_gate)
     n_in = 2 * n_slot
     q_out, q_in = iota((n_in, n_in), 0), iota((n_in, n_in), 1)
     per = NZ * CAP
     want = ((q_out % per) // CAP) * (4 * CAP) + (q_out // per) * CAP + q_out % CAP
     perm = jnp.where(q_in == want, 1.0, 0.0).astype(BF)
-    moved = lax.dot_general(perm, z_in[...].reshape(n_in, WIDE), NN, preferred_element_type=F32)
-    y_out[...] = moved.astype(BF).reshape(y_out.shape)
+
+    def regroup(copies, src, dst):
+        for copy in copies:
+            copy.wait_recv()
+        moved = lax.dot_general(perm, src[...].reshape(n_in, WIDE), NN, preferred_element_type=F32)
+        dst[...] = moved.astype(BF).reshape(dst.shape)
+
+    regroup(z_copies, z_in, y_out)
 
     def spread(src, dst, send, recv):
         copies = {}
@@ -158,10 +177,12 @@
         dst[c, yy] = src[h, c]
         return copies
 
-    opposite = (x + FAR) % NX
-    f_copy = remote(y_out, f_out, fs.at[0], fr.at[0], at(z, y, opposite, c))
     y_copies = spread(y_out, y_in, ys, yr)
     transpose(w_up, t_up)
+    cut_up(1, w_up)
+    cut_up(2, w_down)
+    f_copy.wait_recv()
+    h_copies = to_z(f_out, h_in, hs, hr)
 
     right, left = (x + 1) % NX, (x + NX - 1) % NX
     g_copies, b_copies = {}, {}
@@ -210,17 +231,21 @@
                     forward(j, way, s, m)
                 hand_over(j, s if way == 0 else STEPS + s, target(1 - way, s), m)
 
-    def multiply():
-        for copy in b_copies.values():
-            copy.wait_recv()
-
-        def both(a):
-            return jnp.concatenate([acts[a, j].reshape(NX * chip, LANES) for j in range(2)], axis=1)
-
-        xs, dy = both(0), both(1)
-        gate = lax.dot_general(w_gate[0], xs, NN, preferred_element_type=F32)
-        up = lax.dot_general(w_up[0], xs, NN, preferred_element_type=F32)
-        down = lax.dot_general(w_down[0], dy, NN, preferred_element_type=F32)
+    def add_piece(n, p, first=False):
+        for j in range(2):
+            for m in range(len(G_CUT)):
+                b_copies[j, n, m].wait_recv()
+        for n, a in ((0, 0), (1, 0), (2, 1)):
+            piece = jnp.concatenate([acts[a, 0, p], acts[a, 1, p]], axis=1)
+            res = lax.dot_general(w_cut[n, p], piece, NN, preferred_element_type=F32)
+            pre[n] = res if first else pre[n] + res
+
+    def add_step(s):
+        add_piece(s, target(1, s))
+        add_piece(STEPS + s, target(0, s))
+
+    def gradients():
+        gate, up, down = pre[0], pre[1], pre[2]
         sig = 1.0 / (1.0 + jnp.exp(-gate))
         up_grad = (down * gate * sig).astype(BF)
         gate_grad = (down * up * sig * (1.0 + gate * (1.0 - sig))).astype(BF)
@@ -232,14 +257,15 @@
         fill = jnp.zeros((rows - feat, LANES), F32)
         for n, (way, dist) in enumerate(ORDER):
             d = target(way, dist)
-            res = lax.dot_general(t_gate[d], gate_grad, NN, preferred_element_type=F32)
-            res += lax.dot_general(t_up[d], up_grad, NN, preferred_element_type=F32)
-            for j in range(2):
-                here = res[:, j * LANES:(j + 1) * LANES]
-                low = jnp.concatenate([here[:feat], fill], axis=0)
-                high = jnp.concatenate([here[feat:], fill], axis=0)
-                keep[d, j] = jnp.where(c == 0, low, high)
-                part[d, j] = jnp.where(c == 0, high, low).astype(BF)
+            for side in range(2):
+                res = lax.dot_general(t_gate[d, side], gate_grad, NN, preferred_element_type=F32)
+                res += lax.dot_general(t_up[d, side], up_grad, NN, preferred_element_type=F32)
+                for j in range(2):
+                    here = jnp.concatenate([res[:, j * LANES:(j + 1) * LANES], fill], axis=0)
+                    if side == 0:
+                        keep[d, j] = here
+                    else:
+                        part[d, j] = here.astype(BF)
             p_copies[way, dist] = remote(
                 part.at[d], twin.at[d], ps.at[n], pr.at[n], at(z, y, x, 1 - c)
             )
@@ -298,32 +324,38 @@
             sums.append(total)
         return jnp.concatenate(sums, axis=0)
 
-    prepare(0, y_copies, y_in, x)
-    begin(0)
-    f_copy.wait_recv()
-    f_copies = spread(f_out, f_in, ws, wr)
-    prepare(1, y_copies, y_in, x)
-    begin(1)
+    for j in range(2):
+        prepare(j, y_copies, y_in, x)
+        begin(j)
+    regroup(h_copies, h_in, h_out)
+    f_copies = spread(h_out, f_in, ws, wr)
     for s in range(1, STEPS + 1):
         for j in range(2):
             arrive(j, s)
-        if s == 2:
+        if s == 1:
+            add_piece(0, x, True)
+        elif s == 2:
+            add_step(1)
             for j in range(2):
                 prepare(j, f_copies, f_in, opposite)
                 for m in range(len(G_CUT)):
                     hand_over(j, NX - 1, opposite, m)
-    partials(*multiply())
+    add_step(2)
+    add_piece(NX - 1, opposite)
+    add_step(STEPS)
+    partials(*gradients())
     k_copies = {}
-    for j in range(2):
-        give_back(j, own(j, 0, FAR), far_out, far_in, ks, kr, k_copies)
     for t in range(STEPS):
-        for j in range(2):
+        if t == 1:
+            for j in (1, 0):
+                give_back(j, own(j, 0, FAR), far_out, far_in, ks, kr, k_copies)
+        for j in (1, 0):
             link(j, j, t)
             link(j, 1 - j, t)
     sum_out[...] = collect(far_in, k_copies).astype(BF)
     e_copy = remote(sum_out, sum_in, es.at[0], er.at[0], at(z, y, opposite, c))
     u_copies = {}
-    for j in range(2):
+    for j in (1, 0):
         val = own(j, 0, 0)
         for way in range(2):
             for m in range(len(C_CUT)):
@@ -383,12 +415,16 @@
             pltpu.VMEM((1, hid, width), BF),
             pltpu.VMEM((1, hid, width), BF),
             dma((7,)),
-            pltpu.VMEM((NX, 2 * feat, hid), BF),
-            pltpu.VMEM((NX, 2 * feat, hid), BF),
+            pltpu.VMEM((NX, 2, feat, hid), BF),
+            pltpu.VMEM((NX, 2, feat, hid), BF),
+            pltpu.VMEM((3, NX, hid, 2 * feat), BF),
+            pltpu.VMEM((3, hid, 2 * LANES), F32),
             pltpu.VMEM((NZ, 4 * CAP, WIDE), BF),
             pltpu.VMEM((NZ, 4 * CAP, WIDE), BF),
             pltpu.VMEM((2, 2, NZ * CAP, WIDE), BF),
             pltpu.VMEM((2, NY, NZ * CAP, WIDE), BF),
+            pltpu.VMEM((NZ, 4 * CAP, WIDE), BF),
+            pltpu.VMEM((NZ, 4 * CAP, WIDE), BF),
             pltpu.VMEM((2, 2, NZ * CAP, WIDE), BF),
             pltpu.VMEM((2, NY, NZ * CAP, WIDE), BF),
             pltpu.VMEM((2, 2, NX, 2 * feat, LANES), BF),
@@ -408,6 +444,7 @@
             dma((NZ - 1,)), dma((NZ - 1,)),
             dma((NY, 2)), dma((NY, 2)),
             dma((1,)), dma((1,)),
+            dma((NZ - 1,)), dma((NZ - 1,)),
             dma((NY, 2)), dma((NY, 2)),
             dma((2, 2, STEPS, 2)), dma((2, 2, STEPS, 2)),
             dma((2, NX, 2)), dma((2, NX, 2)),

time: 81.9 us -> 79.1 us (0.966)
  the two profiles are of different devices: /device:TPU:16 before, /device:TPU:14 now
where the time goes in v3:
time: 79.1 us; the launch traced here: 78.9 us
  Pallas kernels  77.5 us (98%)
  local copies, waits for them, and re-layouts  1.32 us (2%)
    pallas_call x1, Pallas kernels, per_device(): pl.pallas_call(kernel, out_shape=jax.ShapeDtypeStruct((n_tok, feat), BF),...  77.5 us

profile of v3, /device:TPU:14, one launch (start us, length us, event | category | flops | bytes accessed | tf_op | source)
XLA Modules:
  0.0 78.9 jit_solution(14656119473803587295)
XLA Ops:
  0.0 77.5 %shard_map.73 = bf16[32,200]{1,0:T(8,128)(2,1)} custom-call(bf16[32,200]{1,0:T(8,128)(2,1)} %tok_hbm.1, bf16[32,200]{1,0:T(8,128)(2,1)} %grd_hbm.1, f32[1,32]{1,0:T(1,128)} %bitcast.2, s32[1,32]{1,0:T(1,128)} %bitcast.3, bf16[1,143,3200]{2,1,0:T(8,128)(2,1)} %gate_hbm.1, bf16[1,143,3200]{2,1,0:T(8,128)(2,1)} %up_hbm.1, bf16[1,143,3200]{2,1,0:T(8,128)(2,1)} %down_hbm.1), custom_call_target="tpu_custom_call" | custom-call | tf_op jit(solution)/shard_map/pallas_call | solution.py:404
  77.5 1.3 %copy.9 = bf16[32,200]{1,0:T(8,128)(2,1)} copy(bf16[32,200]{1,0:T(8,128)(2,1)} %shard_map.73) | data formatting | bytes 25600

commit v4 on v3

--- a/solution.py
+++ b/solution.py
@@ -24,6 +24,7 @@
 C_CUT = (112, 96)
 FAR = NX // 2
 STEPS = 3
+FARTHEST = (4, 3, 5, 2, 6, 1, 7)
 ORDER = ((0, 3), (1, 3), (0, FAR), (0, 2), (1, 2), (0, 1), (1, 1), (0, 0))
 
 
@@ -61,12 +62,18 @@
         started.append(copy)
         return copy
 
+    def drain(most=None):
+        n = len(started) if most is None else most
+        for copy in started[:n]:
+            copy.wait_send()
+        del started[:n]
+
     def y_of(i):
         hh = h if i < HALF else 1 - h
         return hh, (yy + i) % HALF
 
     barrier = pltpu.get_barrier_semaphore()
-    greeted = [at((z + k) % NZ, y, x, c) for k in range(1, NZ)]
+    greeted = [at((z + k) % NZ, y, x, c) for k in FARTHEST]
     for i in range(NY):
         hh, yv = y_of(i)
         if i > 0:
@@ -118,7 +125,7 @@
 
     def to_z(src, dst, send, recv):
         copies = []
-        for k in range(1, NZ):
+        for k in FARTHEST:
             zd = (z + k) % NZ
             copies.append(
                 remote(src.at[zd], dst.at[z], send.at[k - 1], recv.at[k - 1], at(zd, y, x, c))
@@ -164,7 +171,7 @@
 
     def spread(src, dst, send, recv):
         copies = {}
-        for i in range(NY):
+        for i in (1, 3, 2, 0, 4, 5, 7, 6):
             hh, yv = y_of(i)
             for o in range(2):
                 if i == 0 and o == 0:
@@ -301,10 +308,8 @@
     def give_back(j, val, src, dst, send, recv, copies):
         val = jnp.concatenate([val, jnp.zeros((WIDE - rows, LANES), F32)], axis=0)
         src[j] = val.T.astype(BF).reshape(src.shape[1:])
-        for i in range(j * HALF, j * HALF + HALF):
+        for i in ((1, 3, 2), (4, 5, 7, 6))[j]:
             hh, yv = y_of(i)
-            if i == 0:
-                continue
             copies[i] = remote(
                 src.at[j, yv], dst.at[j * HALF + yy], send.at[i], recv.at[i],
                 at(z, hh * HALF + yv, x, c),
@@ -327,6 +332,7 @@
     for j in range(2):
         prepare(j, y_copies, y_in, x)
         begin(j)
+    drain(len(z_copies) + 1 + len(y_copies))
     regroup(h_copies, h_in, h_out)
     f_copies = spread(h_out, f_in, ws, wr)
     for s in range(1, STEPS + 1):
@@ -335,6 +341,7 @@
         if s == 1:
             add_piece(0, x, True)
         elif s == 2:
+            drain(len(h_copies))
             add_step(1)
             for j in range(2):
                 prepare(j, f_copies, f_in, opposite)
@@ -346,6 +353,8 @@
     partials(*gradients())
     k_copies = {}
     for t in range(STEPS):
+        if t == 2:
+            drain()
         if t == 1:
             for j in (1, 0):
                 give_back(j, own(j, 0, FAR), far_out, far_in, ks, kr, k_copies)
@@ -374,12 +383,8 @@
     last_out[...] = lax.dot_general(
         turn, both, NN, precision=lax.Precision.HIGHEST, preferred_element_type=F32
     ).reshape(last_out.shape)
-    v_copies = []
-    for k in range(1, NZ):
-        zd = (z + k) % NZ
-        copy = remote(last_out.at[zd], last_in.at[z], vs.at[k - 1], vr.at[k - 1], at(zd, y, x, c))
-        v_copies.append(copy)
-    last_in[z] = last_out[z]
+    v_copies = to_z(last_out, last_in, vs, vr)
+    drain(len(started) - len(v_copies))
     pick = jnp.where(slot_col == iota((n_tok, n_slot), 1).astype(F32), 1.0, 0.0)
     for copy in v_copies:
         copy.wait_recv()
@@ -389,8 +394,7 @@
     )
     out[...] = (w_col * got[:, :feat]).astype(BF)
 
-    for copy in started:
-        copy.wait_send()
+    drain()
 
 
 def per_device(tokens, grad_out, route_weight, routes, gate_weight, up_weight, down_weight):

time: 79.1 us -> 78.5 us (level)
  no operation moved by 1% of the time
where the time goes in v4:
time: 78.5 us; the launch traced here: 78.1 us
  Pallas kernels  76.8 us (98%)
  local copies, waits for them, and re-layouts  1.32 us (2%)
    pallas_call x1, Pallas kernels, per_device(): pl.pallas_call(kernel, out_shape=jax.ShapeDtypeStruct((n_tok, feat), BF),...  76.8 us

profile of v4, /device:TPU:14, one launch (start us, length us, event | category | flops | bytes accessed | tf_op | source)
XLA Modules:
  0.0 78.1 jit_solution(5817769059942813568)
XLA Ops:
  0.0 76.8 %shard_map.73 = bf16[32,200]{1,0:T(8,128)(2,1)} custom-call(bf16[32,200]{1,0:T(8,128)(2,1)} %tok_hbm.1, bf16[32,200]{1,0:T(8,128)(2,1)} %grd_hbm.1, f32[1,32]{1,0:T(1,128)} %bitcast.2, s32[1,32]{1,0:T(1,128)} %bitcast.3, bf16[1,143,3200]{2,1,0:T(8,128)(2,1)} %gate_hbm.1, bf16[1,143,3200]{2,1,0:T(8,128)(2,1)} %up_hbm.1, bf16[1,143,3200]{2,1,0:T(8,128)(2,1)} %down_hbm.1), custom_call_target="tpu_custom_call" | custom-call | tf_op jit(solution)/shard_map/pallas_call | solution.py:408
  76.8 1.3 %copy.9 = bf16[32,200]{1,0:T(8,128)(2,1)} copy(bf16[32,200]{1,0:T(8,128)(2,1)} %shard_map.73) | data formatting | bytes 25600
